TPU v7x, 32 devices: a whole 2x2x4 slice. The times are simulated.
32 devices in a mesh: wide: 8 (over z, x), blk: 4 (over y, core).
Axes of the slice: x: 2, y: 2, z: 4, core: 2. Of those that a mesh axis runs over, the one named last changes fastest.
Arguments:
- tokens: bfloat16 [64, 512, 768], P('wide', 'blk'), may hold values from -6 to 6
- lengths: int32 [64, 7], P('wide'), may hold values from 0 to 512, as said below
- query_weight: bfloat16 [768, 768], replicated, may hold values from -0.4375 to 0.4375
- query_bias: bfloat16 [768], replicated, may hold values from -3 to 3
- key_weight: bfloat16 [768, 768], replicated, may hold values from -0.21875 to 0.21875
- value_weight: bfloat16 [768, 768], replicated, may hold values from -0.21875 to 0.21875
- value_bias: bfloat16 [768], replicated, may hold values from -3 to 3
- out_weight: bfloat16 [768, 768], replicated, may hold values from -0.75 to 0.75
- out_bias: bfloat16 [768], replicated, may hold values from -2 to 2
- first_gain: bfloat16 [768], replicated, may hold values from 0.099609375 to 1.8984375
- first_shift: bfloat16 [768], replicated, may hold values from -2 to 2
- inner_weight: bfloat16 [768, 3072], replicated, may hold values from -0.21875 to 0.21875
- inner_bias: bfloat16 [3072], replicated, may hold values from -3 to 3
- outer_weight: bfloat16 [3072, 768], replicated, may hold values from -0.109375 to 0.109375
- outer_bias: bfloat16 [768], replicated, may hold values from -2 to 2
- second_gain: bfloat16 [768], replicated, may hold values from 0.099609375 to 1.8984375
- second_shift: bfloat16 [768], replicated, may hold values from -2 to 2
- cotangent: bfloat16 [64, 512, 768], P('wide', 'blk'), may hold values from -6 to 6
Outputs:
- output: bfloat16 [64, 512, 768], P('wide', 'blk')
- grad_tokens: bfloat16 [64, 512, 768], P('wide', 'blk')
- grad_query_weight: float32 [768, 768], replicated
- grad_query_bias: float32 [768], replicated
- grad_key_weight: float32 [768, 768], replicated
- grad_value_weight: float32 [768, 768], replicated
- grad_value_bias: float32 [768], replicated
- grad_out_weight: float32 [768, 768], replicated
- grad_out_bias: float32 [768], replicated
- grad_first_gain: float32 [768], replicated
- grad_first_shift: float32 [768], replicated
- grad_inner_weight: float32 [768, 3072], replicated
- grad_inner_bias: float32 [3072], replicated
- grad_outer_weight: float32 [3072, 768], replicated
- grad_outer_bias: float32 [768], replicated
- grad_second_gain: float32 [768], replicated
- grad_second_shift: float32 [768], replicated
Inputs may be any that keep to these rules, and one draw needn't show every extreme that they name: Each row's 7 lengths sum to 512; entries may be zero; the fourth one is a document that starts within the first 128 tokens of its row and ends within the last 128; some row holds a single document of all 512 tokens.
All inputs are finite; a program needn't handle non-finite values.
Results may differ from a plain program's by a relative error of at most 0.02.
Values may be sent and summed in bfloat16 or wider, within the bound.
No kernel may reach another device: no remote copies, remote signals or barrier semaphores. Data moves between devices by JAX's collectives and lax.ppermute only.
A program may use at most 256 MiB of HBM per device.

v0:
```python
import jax
import jax.numpy as jnp
from jax import lax
from jax.sharding import PartitionSpec as P

HEADS = 12


NEG = -1e30


def norm_layer(value, gain, shift):
    center = value - jnp.mean(value, axis=-1, keepdims=True)
    spread = jnp.mean(center * center, axis=-1, keepdims=True)
    return center * lax.rsqrt(spread + 1e-12) * gain + shift


def gelu_exact(value):
    return jax.nn.gelu(value, approximate=False)


def segment_ids(lengths, first, count):
    ends = jnp.cumsum(lengths, axis=-1)
    place = first + jnp.arange(count, dtype=jnp.int32)
    return jnp.sum((place[None, :, None] >= ends[:, None, :]).astype(jnp.int32), axis=-1)


def matmul(left, right):
    return jnp.dot(left, right, preferred_element_type=jnp.float32)


def pack_all(grads, parts):
    flat = jnp.concatenate([item.reshape(-1) for item in grads])
    extra = -flat.shape[0] % parts
    flat = jnp.concatenate([flat, jnp.zeros((extra,), jnp.float32)])
    return flat.reshape(parts, -1)


def unpack_all(packed, shapes):
    flat = packed.reshape(-1)
    pieces = []
    offset = 0
    for shape in shapes:
        length = 1
        for extent in shape:
            length = length * extent
        pieces.append(flat[offset : offset + length].reshape(shape))
        offset = offset + length
    return pieces


def per_device(
    tokens,
    lengths,
    query_weight,
    query_bias,
    key_weight,
    value_weight,
    value_bias,
    out_weight,
    out_bias,
    first_gain,
    first_shift,
    inner_weight,
    inner_bias,
    outer_weight,
    outer_bias,
    second_gain,
    second_shift,
    cotangent,
):
    rows, width, model = tokens.shape
    heads = HEADS
    head_dim = model // heads
    scale = head_dim ** (-0.5)
    count = rows * width
    seg_local = segment_ids(lengths, lax.axis_index("blk") * width, width)
    flat = tokens.reshape(count, model)
    query = (matmul(flat, query_weight) + query_bias.astype(jnp.float32)).astype(jnp.bfloat16)
    keys = matmul(flat, key_weight).astype(jnp.bfloat16)
    values = (matmul(flat, value_weight) + value_bias.astype(jnp.float32)).astype(jnp.bfloat16)
    pairs = jnp.stack([keys.reshape(rows, width, model), values.reshape(rows, width, model)])
    query_heads = query.reshape(rows, width, heads, head_dim)

    def scores_of(piece, start):
        span = piece.shape[2]
        key_heads = piece[0].reshape(rows, span, heads, head_dim)
        raw = (
            jnp.einsum(
                "rqhd,rkhd->rqhk", query_heads, key_heads, preferred_element_type=jnp.float32
            )
            * scale
        )
        seg_keys = segment_ids(lengths, start, span)
        allowed = seg_local[:, :, None, None] == seg_keys[:, None, None, :]
        return (raw, allowed, key_heads, piece[1].reshape(rows, span, heads, head_dim))

    best = jnp.full((rows, width, heads), NEG, jnp.float32)
    raw, allowed, key_heads, value_heads = scores_of(
        lax.all_gather(pairs, "blk", axis=2, tiled=True), jnp.int32(0)
    )
    high = jnp.maximum(best, jnp.max(jnp.where(allowed, raw, NEG), axis=-1))
    weights = jnp.where(allowed, jnp.exp(jnp.where(allowed, raw - high[..., None], NEG)), 0.0)
    part = jnp.einsum(
        "rqhk,rkhd->rqhd",
        weights.astype(jnp.bfloat16),
        value_heads,
        preferred_element_type=jnp.float32,
    )
    total = jnp.sum(weights, axis=-1)
    context = part / total[..., None]
    lse = high + jnp.log(total)
    context_low = context.reshape(count, model).astype(jnp.bfloat16)
    attn = matmul(context_low, out_weight) + out_bias.astype(jnp.float32)
    z_first = flat.astype(jnp.float32) + attn
    first, pull_first = jax.vjp(
        norm_layer, z_first, first_gain.astype(jnp.float32), first_shift.astype(jnp.float32)
    )
    first_low = first.astype(jnp.bfloat16)
    hidden = matmul(first_low, inner_weight) + inner_bias.astype(jnp.float32)
    gelled, pull_gelu = jax.vjp(gelu_exact, hidden)
    gelled_low = gelled.astype(jnp.bfloat16)
    mixed = matmul(gelled_low, outer_weight) + outer_bias.astype(jnp.float32)
    result, pull_second = jax.vjp(
        norm_layer, first + mixed, second_gain.astype(jnp.float32), second_shift.astype(jnp.float32)
    )
    output = result.reshape(rows, width, model).astype(jnp.bfloat16)
    grad_out = cotangent.reshape(count, model).astype(jnp.float32)
    grad_z2, grad_g2, grad_e2 = pull_second(grad_out)
    grad_mixed = grad_z2.astype(jnp.bfloat16)
    grad_w2 = matmul(gelled_low.T, grad_mixed)
    grad_c2 = jnp.sum(grad_mixed.astype(jnp.float32), axis=0)
    (grad_hidden,) = pull_gelu(matmul(grad_mixed, outer_weight.T))
    grad_hidden = grad_hidden.astype(jnp.bfloat16)
    grad_w1 = matmul(first_low.T, grad_hidden)
    grad_c1 = jnp.sum(grad_hidden.astype(jnp.float32), axis=0)
    grad_first = grad_z2 + matmul(grad_hidden, inner_weight.T)
    grad_z1, grad_g1, grad_e1 = pull_first(grad_first)
    grad_attn = grad_z1.astype(jnp.bfloat16)
    grad_wo = matmul(context_low.T, grad_attn)
    grad_bo = jnp.sum(grad_attn.astype(jnp.float32), axis=0)
    grad_context = (
        matmul(grad_attn, out_weight.T).astype(jnp.bfloat16).reshape(rows, width, heads, head_dim)
    )
    delta = jnp.sum(grad_context.astype(jnp.float32) * context, axis=-1)
    piece = lax.all_gather(pairs, "blk", axis=2, tiled=True)
    span = piece.shape[2]
    raw, allowed, key_heads, value_heads = scores_of(piece, jnp.int32(0))
    probs = jnp.where(allowed, jnp.exp(jnp.where(allowed, raw - lse[..., None], NEG)), 0.0)
    grad_probs = jnp.einsum(
        "rqhd,rkhd->rqhk", grad_context, value_heads, preferred_element_type=jnp.float32
    )
    grad_raw = (probs * (grad_probs - delta[..., None])).astype(jnp.bfloat16)
    grad_query = scale * jnp.einsum(
        "rqhk,rkhd->rqhd", grad_raw, key_heads, preferred_element_type=jnp.float32
    )
    grad_keys = scale * jnp.einsum(
        "rqhk,rqhd->rkhd", grad_raw, query_heads, preferred_element_type=jnp.float32
    )
    grad_values = jnp.einsum(
        "rqhk,rqhd->rkhd",
        probs.astype(jnp.bfloat16),
        grad_context,
        preferred_element_type=jnp.float32,
    )
    block = jnp.stack(
        [grad_keys.reshape(rows, span, model), grad_values.reshape(rows, span, model)]
    )
    grad_pairs = block
    grad_query, grad_pairs = (grad_query, grad_pairs)
    own_pairs = lax.psum_scatter(
        grad_pairs.astype(jnp.bfloat16), "blk", scatter_dimension=2, tiled=True
    ).astype(jnp.float32)
    grad_q = grad_query.reshape(count, model).astype(jnp.bfloat16)
    grad_k = own_pairs[0].reshape(count, model).astype(jnp.bfloat16)
    grad_v = own_pairs[1].reshape(count, model).astype(jnp.bfloat16)
    grad_wq = matmul(flat.T, grad_q)
    grad_bq = jnp.sum(grad_q.astype(jnp.float32), axis=0)
    grad_wk = matmul(flat.T, grad_k)
    grad_wv = matmul(flat.T, grad_v)
    grad_bv = jnp.sum(grad_v.astype(jnp.float32), axis=0)
    grad_in = (
        grad_z1
        + matmul(grad_q, query_weight.T)
        + matmul(grad_k, key_weight.T)
        + matmul(grad_v, value_weight.T)
    )
    grad_tokens = grad_in.reshape(rows, width, model).astype(jnp.bfloat16)
    grads = (
        grad_wq,
        grad_bq,
        grad_wk,
        grad_wv,
        grad_bv,
        grad_wo,
        grad_bo,
        grad_g1,
        grad_e1,
        grad_w1,
        grad_c1,
        grad_w2,
        grad_c2,
        grad_g2,
        grad_e2,
    )
    shapes = [item.shape for item in grads]
    packed = pack_all(grads, lax.axis_size("wide") * lax.axis_size("blk"))
    mine = lax.psum_scatter(packed, ("wide", "blk"), scatter_dimension=0, tiled=True)
    full = lax.all_gather(mine.astype(jnp.bfloat16), ("wide", "blk"), axis=0, tiled=True).astype(
        mine.dtype
    )
    summed_grads = unpack_all(full, shapes)
    return (output, grad_tokens) + tuple(summed_grads)


def solution(mesh):
    placed = (
        P("wide", "blk", None),
        P("wide", None),
        P(),
        P(),
        P(),
        P(),
        P(),
        P(),
        P(),
        P(),
        P(),
        P(),
        P(),
        P(),
        P(),
        P(),
        P(),
        P("wide", "blk", None),
    )
    return jax.shard_map(
        per_device,
        mesh=mesh,
        in_specs=placed,
        out_specs=(
            P("wide", "blk", None),
            P("wide", "blk", None),
            P(),
            P(),
            P(),
            P(),
            P(),
            P(),
            P(),
            P(),
            P(),
            P(),
            P(),
            P(),
            P(),
            P(),
            P(),
        ),
        check_vma=False,
    )
```

profile of v0, /device:TPU:0, one launch (start us, length us, event | category | flops | bytes accessed | tf_op | source)
XLA Modules:
  0.0 1780.1 jit_solution(2691409391525041229)
XLA Ops:
  25.2 74.5 %all-gather.4.cloned.1.call-done = bf16[2,8,512,768]{3,2,1,0:T(8,128)(2,1)} async-done(((bf16[2,8,128,768]{3,2,1,0:T(8,128)(2,1)}), bf16[2,8,512,768]{3,2,1,0:T(8,128)(2,1)}) %all-gather.4.cloned.1.call-update) | async-done | bytes 12582928 | tf_op jit(solution)/shard_map/all_gather | solution.py:100
  99.7 10.3 fusion.71
  110.0 8.8 copy.86
  118.8 12.9 fusion.2
  140.3 11.9 fusion.10
  152.9 18.8 %fusion.72 = (bf16[8,128,12,64]{1,3,2,0:T(8,128)(2,1)S(1)}, f32[8,128,12,64]{1,3,2,0:T(8,128)}) fusion(f32[8,128,12]{1,2,0:T(8,128)S(1)} %fusion.10, bf16[8,512,12,64]{1,3,2,0:T(8,128)(2,1)} %bitcast.156, f32[8,12,512,128]{3,2,1,0:T(8,128)} %get-tuple-element.50, f32[8,128,12]{1,2,0:T(8,128)S(1)} %broadcast_maximum_fusion, ...), kind=kOutput, calls=%fused_computation.143 | convolution fusion | flops 838336512 | bytes 36798464 | tf_op jit(solution)/shard_map/rqhk,rkhd->rqhd/dot_general | solution.py:104
  176.0 35.1 %multiply_convert_fusion.1 = (bf16[1024,3072]{1,0:T(8,128)(2,1)S(1)}, f32[1024,3072]{1,0:T(8,128)}, f32[1024,3072]{1,0:T(8,128)}) fusion(f32[3072]{0:T(1024)S(1)} %convert_element_type.172, bf16[768,3072]{1,0:T(8,128)(2,1)S(1)} %bitcast.179, f32[1024,768]{1,0:T(8,128)S(1)} %get-tuple-element.54, f32[768]{0:T(1024)S(1)} %convert_element_type.170, ...), kind=kOutput, calls=%fused_computation.25 | convolution fusion | flops 5043388416 | bytes 39348224 | tf_op jit(solution)/shard_map/dot_general | solution.py:29
  225.0 17.9 %convert_reduce_fusion.1 = (f32[3072]{0:T(1024)}, bf16[1024,3072]{1,0:T(8,128)(2,1)}) fusion(f32[1024,3072]{1,0:T(8,128)} %get-tuple-element.33, bf16[1024,768]{1,0:T(8,128)(2,1)S(1)} %get-tuple-element.23, bf16[3072,768]{1,0:T(8,128)(2,1)} %param.31, f32[1024,3072]{1,0:T(8,128)} %get-tuple-element.55, f32[3072]{0:T(1024)S(1)} %convert_element_type.172), kind=kOutput, calls=%fused_computation.21 | convolution fusion | flops 4885312512 | bytes 37773312 | tf_op jit(solution)/shard_map/dot_general | solution.py:29
  242.9 10.6 multiply_reduce_fusion
  264.6 13.7 fusion.28
  278.4 8.9 copy.101
  289.9 20.6 %fusion.1 = bf16[8,128,12,512]{1,3,2,0:T(8,128)(2,1)} fusion(f32[8,12,512,128]{3,2,1,0:T(8,128)} %get-tuple-element.50, f32[8,128,12]{1,2,0:T(8,128)S(1)} %multiply_reduce_fusion.1, f32[8,128,12]{1,2,0:T(8,128)S(1)} %copy-done.26, pred[8,128,512]{1,2,0:T(8,128)(4,1)S(1)} %copy-done.15, bf16[8,512,12,64]{1,3,2,0:T(8,128)(2,1)} %bitcast.157, ...), kind=kOutput, calls=%fused_computation.3 | convolution fusion | flops 849346560 | bytes 46235648 | tf_op jit(solution)/shard_map/rqhd,rkhd->rqhk/dot_general | solution.py:150
  310.5 11.7 multiply_convert_fusion
  322.2 8.7 copy.100
  330.9 10.7 pad_maximum_fusion
  343.3 10.6 convert_reduce_fusion.6
  370.2 9.2 convolution_bitcast_fusion
  385.4 10.1 fusion.76
  395.5 10.8 reshape.205
  411.1 29.7 %reduce-scatter.2.cloned.1.call-done = bf16[2,8,128,768]{3,2,1,0:T(8,128)(2,1)} async-done(((bf16[2,8,512,768]{3,2,1,0:T(8,128)(2,1)}), bf16[2,8,128,768]{3,2,1,0:T(8,128)(2,1)}) %reduce-scatter.2.cloned.1.call-update) | async-done | bytes 3145744 | tf_op jit(solution)/shard_map/reduce_scatter | solution.py:171
  465.0 21.2 %dynamic-update-slice.2 = f32[7087104]{0:T(1024)} dynamic-update-slice(f32[7087104]{0:T(1024)} %constant_dynamic-update-slice_fusion.8, f32[589824]{0:T(1024)} %reshape.201, s32[]{} %constant.106) | dynamic-update-slice | bytes 4718596
  486.1 21.2 %dynamic-update-slice.3 = f32[7087104]{0:T(1024)} dynamic-update-slice(f32[7087104]{0:T(1024)} %dynamic-update-slice.2, f32[589824]{0:T(1024)} %reshape.202, s32[]{} %constant.107) | dynamic-update-slice | bytes 4718596
  508.6 20.2 %dynamic-update-slice.5 = f32[7087104]{0:T(1024)} dynamic-update-slice(f32[7087104]{0:T(1024)} %constant_dynamic-update-slice_fusion.7, f32[589824]{0:T(1024)S(1)} %reshape.203, s32[]{} %constant.109) | dynamic-update-slice | bytes 4718596
  532.7 80.6 %dynamic-update-slice.9 = f32[7087104]{0:T(1024)} dynamic-update-slice(f32[7087104]{0:T(1024)} %constant_dynamic-update-slice_fusion.4, f32[2359296]{0:T(1024)} %bitcast.153, s32[]{} %constant.113) | dynamic-update-slice | bytes 18874372
  614.7 80.7 %dynamic-update-slice.11 = f32[7087104]{0:T(1024)} dynamic-update-slice(f32[7087104]{0:T(1024)} %constant_dynamic-update-slice_fusion.3, f32[2359296]{0:T(1024)} %reshape.205, s32[]{} %constant.115) | dynamic-update-slice | bytes 18874372
  699.3 37.7 %reshape.206 = f32[32,221472]{1,0:T(8,128)} reshape(f32[7087104]{0:T(1024)} %constant_dynamic-update-slice_fusion) | data formatting | bytes 56696832 | tf_op jit(solution)/shard_map/reshape | solution.py:36
  736.9 456.2 %all-reduce.2 = bf16[32,221472]{1,0:T(8,128)(2,1)} all-reduce(f32[32,221472]{1,0:T(8,128)} %reshape.206), channel_id=3, replica_groups=mesh['wide'=8,'blk'=4] {'wide','blk'}, use_global_device_ids=true, to_apply=%region_24.25.clone | all-reduce | flops 7087104 | bytes 42522624
  1203.6 160.8 %all-gather.6.cloned.1.call-done = bf16[32,1,221472]{2,1,0:T(2,128)(2,1)} async-done(((bf16[1,1,221472]{2,1,0:T(2,128)(2,1)}), bf16[32,1,221472]{2,1,0:T(2,128)(2,1)}) %all-gather.6.cloned.1.call-update) | async-done | bytes 14174224 | tf_op jit(solution)/shard_map/all_gather | solution.py:209
  1364.4 303.5 %convert_reduce_fusion = f32[32,221472]{1,0:T(8,128)} fusion(bf16[32,1,221472]{2,1,0:T(2,128)(2,1)} %all-gather.6.cloned.1.call-done), kind=kLoop, calls=%fused_computation | loop fusion | flops 7087104 | bytes 42522624 | tf_op jit(solution)/shard_map/convert_element_type | solution.py:209
  1667.9 36.6 %reshape.217 = f32[7087104]{0:T(1024)} reshape(f32[32,221472]{1,0:T(8,128)} %convert_reduce_fusion) | data formatting | bytes 56696832
  1704.5 31.3 %slice.70 = f32[9228,768]{1,0:T(8,128)} reshape(f32[7087104]{0:T(1024)} %reshape.217) | data formatting | bytes 56696832 | tf_op jit(solution)/shard_map/slice | solution.py:47
  1762.4 11.0 reshape.208
  (208 shorter events, 159.2 us)
Async XLA Ops:
  7.2 165.7 %copy-start = (bf16[768,768]{1,0:T(8,128)(2,1)S(1)}, bf16[768,768]{1,0:T(8,128)(2,1)}, u32[]{:S(2)}) copy-start(bf16[768,768]{1,0:T(8,128)(2,1)} %param.25) | copy-start | bytes 3538948
  7.2 92.5 %all-gather.4.cloned.1.call-start = ((), (), s32[]{:S(2)}) async-start(), calls=%async_computation.1 | async-start | bytes 15728640 | tf_op jit(solution)/shard_map/all_gather | solution.py:100
  8.0 3.3 copy-start.24
  8.0 3.3 copy-start.47
  14.7 426.1 %reduce-scatter.2.cloned.1.call-start = ((), (), s32[]{:S(2)}) async-start(), calls=%async_computation.2 | async-start | bytes 15728640 | tf_op jit(solution)/shard_map/reduce_scatter | solution.py:171
  19.4 3.5 copy-start.43
  19.4 3.5 copy-start.44
  19.4 3.6 copy-start.45
  19.4 4.2 copy-start.46
  22.9 95.9 %copy-start.5 = (bf16[96,8,8,128]{3,2,1,0:T(8,128)(2,1)}, bf16[96,8,8,128]{3,2,1,0:T(8,128)(2,1)S(1)}, u32[]{:S(2)}) copy-start(bf16[96,8,8,128]{3,2,1,0:T(8,128)(2,1)S(1)} %copy.109) | copy-start | bytes 4718596
  25.1 127.7 %copy-start.14 = (pred[8,128,512]{1,2,0:T(8,128)(4,1)}, pred[8,128,512]{1,2,0:T(8,128)(4,1)S(1)}, u32[]{:S(2)}) copy-start(pred[8,128,512]{1,2,0:T(8,128)(4,1)S(1)} %broadcast_compare_fusion) | copy-start | bytes 1572868
  173.1 38.0 %slice-start = ((s8[4718592]{0:T(1024)(128)(4,1)}), s8[4194304]{0:T(1024)(128)(4,1)S(1)}, s32[]{:S(2)}) async-start(s8[4718592]{0:T(1024)(128)(4,1)} %bitcast.176), calls=%async_computation.4 | async-start | bytes 8388608
  174.8 78.7 %copy-start.2 = (f32[1024,768]{1,0:T(8,128)}, f32[1024,768]{1,0:T(8,128)S(1)}, u32[]{:S(2)}) copy-start(f32[1024,768]{1,0:T(8,128)S(1)} %get-tuple-element.54) | copy-start | bytes 9437188
  176.0 35.2 %copy-start.36 = (f32[768]{0:T(1024)S(1)}, f32[768]{0:T(1024)}, u32[]{:S(2)}) copy-start(f32[768]{0:T(1024)} %convert_element_type.174) | copy-start | bytes 9220
  176.0 35.2 %slice-start.1 = ((s8[4718592]{0:T(1024)(128)(4,1)}), s8[524288]{0:T(1024)(128)(4,1)S(1)}, s32[]{:S(2)}) async-start(s8[4718592]{0:T(1024)(128)(4,1)} %bitcast.176), calls=%async_computation.5 | async-start | bytes 1048576
  211.1 5.5 copy-start.54
  225.0 17.9 %copy-start.21 = (bf16[1024,768]{1,0:T(8,128)(2,1)}, bf16[1024,768]{1,0:T(8,128)(2,1)S(1)}, u32[]{:S(2)}) copy-start(bf16[1024,768]{1,0:T(8,128)(2,1)S(1)} %get-tuple-element.23) | copy-start | bytes 4718596
  261.2 3.4 copy-start.15
  261.2 3.4 copy-start.26
  278.4 8.9 copy-start.12
  289.9 20.6 %copy-start.6 = (bf16[96,8,8,128]{3,2,1,0:T(8,128)(2,1)S(1)}, bf16[96,8,8,128]{3,2,1,0:T(8,128)(2,1)}, u32[]{:S(2)}) copy-start(bf16[96,8,8,128]{3,2,1,0:T(8,128)(2,1)} %copy-done.5) | copy-start | bytes 4718596
  341.6 1022.8 %all-gather.6.cloned.1.call-start = ((), (), s32[]{:S(2)}) async-start(), calls=%async_computation.3 | async-start | bytes 29246976 | tf_op jit(solution)/shard_map/all_gather | solution.py:209
  379.4 6.0 copy-start.22
  507.3 21.5 %copy-start.31 = (f32[768]{0:T(1024)S(1)}, f32[768]{0:T(1024)}, u32[]{:S(2)}) copy-start(f32[768]{0:T(1024)} %get-tuple-element.24) | copy-start | bytes 9220
  507.3 22.8 %copy-start.39 = (f32[768]{0:T(1024)S(1)}, f32[768]{0:T(1024)}, u32[]{:S(2)}) copy-start(f32[768]{0:T(1024)} %get-tuple-element.17) | copy-start | bytes 9220
  507.3 24.1 %copy-start.38 = (f32[768]{0:T(1024)S(1)}, f32[768]{0:T(1024)}, u32[]{:S(2)}) copy-start(f32[768]{0:T(1024)} %get-tuple-element.21) | copy-start | bytes 9220
  532.7 80.6 %copy-start.34 = (f32[3072]{0:T(1024)S(1)}, f32[3072]{0:T(1024)}, u32[]{:S(2)}) copy-start(f32[3072]{0:T(1024)} %get-tuple-element.61) | copy-start | bytes 36868
  614.7 80.7 %copy-start.30 = (f32[768]{0:T(1024)S(1)}, f32[768]{0:T(1024)}, u32[]{:S(2)}) copy-start(f32[768]{0:T(1024)} %get-tuple-element.22) | copy-start | bytes 9220
  614.7 82.0 %copy-start.33 = (f32[768]{0:T(1024)S(1)}, f32[768]{0:T(1024)}, u32[]{:S(2)}) copy-start(f32[768]{0:T(1024)} %get-tuple-element.19) | copy-start | bytes 9220
  736.9 459.5 %copy-start.18 = (bf16[8,128,12,64]{1,0,3,2:T(8,128)(2,1)S(1)}, bf16[8,128,12,64]{1,0,3,2:T(8,128)(2,1)}, u32[]{:S(2)}) copy-start(bf16[8,128,12,64]{1,0,3,2:T(8,128)(2,1)} %copy-done.17) | copy-start | bytes 4718596
  736.9 459.5 %copy-start.52 = (bf16[768,768]{1,0:T(8,128)(2,1)S(1)}, bf16[768,768]{1,0:T(8,128)(2,1)}, u32[]{:S(2)}) copy-start(bf16[768,768]{1,0:T(8,128)(2,1)} %param.20) | copy-start | bytes 3538948
  1762.4 11.0 copy-start.1
  (30 other events, 56.0 us)
Sparse Core Ops, SparseCore 0:
  14.8 84.7 all-gather.3
  341.8 99.0 reduce-scatter.1
  1196.5 167.8 all-gather.5
where the time goes:
time: 1810 us; the launch traced here: 1780 us
  local copies, waits for them, and re-layouts  490 us (27%)
  blocking collectives  456 us (25%)
  other arithmetic  346 us (19%)
  waiting for transfers between devices  265 us (15%)
  matrix products  208 us (11%)
    unnamed x1, blocking collectives  456 us
    convert_element_type x1, other arithmetic, per_device(): lax.all_gather(mine.astype(jnp.bfloat16), ('wide', 'blk'), axis=0, tiled=...  303 us
    unnamed x137, local copies, waits for them, and re-layouts  300 us
    all_gather x1, waiting for transfers between devices, per_device(): lax.all_gather(mine.astype(jnp.bfloat16), ('wide', 'blk'), axis=0, tiled=...  161 us
    dot_general x18, matrix products, matmul(): return jnp.dot(left, right, preferred_element_type=jnp.float32)  119 us
    all_gather x1, waiting for transfers between devices, per_device(): lax.all_gather(pairs, 'blk', axis=2, tiled=True)  74.5 us
    slice x6, local copies, waits for them, and re-layouts, unpack_all(): pieces.append(flat[offset:offset + length].reshape(shape))  57.9 us
    reshape x1, local copies, waits for them, and re-layouts, pack_all(): return flat.reshape(parts, -1)  37.7 us
  transfers between devices with their start and end apart: 3, of which 3 were waited for; matrix products, arithmetic and copies ran while one was open for 5% of the time, Pallas kernels for 0%

commit v1 on v0

v1 whole, which is shorter than its diff:
```python
import functools

import jax
import jax.numpy as jnp
from jax import lax
from jax.experimental import pallas as pl
from jax.experimental.pallas import tpu as pltpu
from jax.sharding import PartitionSpec as P

HEADS = 12
BIG = 1e30
VMEM_LIMIT = 56 * 1024 * 1024
BF = jnp.bfloat16
F32 = jnp.float32


def swap(value, axis, mask):
    size = lax.axis_size(axis)
    return lax.ppermute(value, axis, [(i, i ^ mask) for i in range(size)])


def matmul(left, right):
    return jnp.dot(left, right, preferred_element_type=F32)


def dot_nt(left, right):
    return lax.dot_general(left, right, (((1,), (1,)), ((), ())), preferred_element_type=F32)


def dot_tn(left, right):
    return lax.dot_general(left, right, (((0,), (0,)), ((), ())), preferred_element_type=F32)


def attn_fwd_kernel(q_ref, k_ref, v_ref, e_ref, f_ref, ctx_ref, qb_ref):
    lane = lax.broadcasted_iota(jnp.int32, (1, 128), 1)
    q = q_ref[0] * BF(0.125)
    k = k_ref[0]
    v = v_ref[0]
    e = e_ref[0]
    f = f_ref[0]
    outs = []
    for h in range(2):
        mine = (lane >= 64) if h else (lane < 64)
        other = 0 if h else 64
        qa = jnp.where(mine, q, e)
        ka = jnp.where(mine, k, f)
        va = jnp.where(mine, v, BF(1.0))
        s = dot_nt(qa, ka)
        high = jnp.max(s, axis=-1, keepdims=True)
        p = jnp.exp(s - high).astype(BF)
        o = matmul(p, va)
        total = o[:, other : other + 1]
        outs.append(o * (1.0 / total))
        lse = high + jnp.log(total)
        hi = lse.astype(BF)
        rest = lse - hi.astype(F32)
        mid = rest.astype(BF)
        low = (rest - mid.astype(F32)).astype(BF)
        qb = jnp.where(lane == other + 8, hi, qa)
        qb = jnp.where(lane == other + 9, mid, qb)
        qb_ref[0, h] = jnp.where(lane == other + 10, low, qb)
    ctx_ref[0] = jnp.where(lane < 64, outs[0], outs[1]).astype(BF)


def attn_bwd_kernel(qb_ref, k_ref, v_ref, f_ref, dctx_ref, ctx_ref, dq_ref, dk_ref, dv_ref):
    lane = lax.broadcasted_iota(jnp.int32, (1, 128), 1)
    k = k_ref[0]
    v = v_ref[0]
    f = f_ref[0]
    dctx = dctx_ref[0]
    prod = dctx.astype(F32) * ctx_ref[0].astype(F32)
    dqs, dks, dvs = [], [], []
    for h in range(2):
        mine = (lane >= 64) if h else (lane < 64)
        other = 0 if h else 64
        delta = jnp.sum(jnp.where(mine, prod, 0.0), axis=-1, keepdims=True)
        hi = delta.astype(BF)
        low = (delta - hi.astype(F32)).astype(BF)
        zero = BF(0.0)
        da = jnp.where(mine, dctx, jnp.where(lane == other, hi, jnp.where(lane == other + 1, low, zero)))
        va = jnp.where(mine, v, jnp.where((lane == other) | (lane == other + 1), BF(-1.0), zero))
        kb = jnp.where(mine, k, f)
        qb = qb_ref[0, h]
        st = dot_nt(kb, qb)
        pt = jnp.exp(st)
        dpt = dot_nt(va, da)
        dst = (pt * dpt).astype(BF)
        dvs.append(matmul(pt.astype(BF), da))
        dks.append(matmul(dst, qb))
        dqs.append(dot_tn(dst, k))
    dq_ref[0] = (jnp.where(lane < 64, dqs[0], dqs[1]) * 0.125).astype(BF)
    dk_ref[0] = jnp.where(lane < 64, dks[0], dks[1]).astype(BF)
    dv_ref[0] = jnp.where(lane < 64, dvs[0], dvs[1]).astype(BF)


def attn_forward(q, k, v, e, f):
    rows, seq, model = q.shape
    pairs = model // 128
    wide = pl.BlockSpec((1, seq, 128), lambda r, p: (r, 0, p))
    mask = pl.BlockSpec((1, seq, 128), lambda r, p: (r, 0, 0))
    return pl.pallas_call(
        attn_fwd_kernel,
        grid=(rows, pairs),
        in_specs=[wide, wide, wide, mask, mask],
        out_specs=[wide, pl.BlockSpec((1, 2, seq, 128), lambda r, p: (r, p, 0, 0))],
        out_shape=[
            jax.ShapeDtypeStruct((rows, seq, model), BF),
            jax.ShapeDtypeStruct((rows, 2 * pairs, seq, 128), BF),
        ],
        compiler_params=pltpu.CompilerParams(vmem_limit_bytes=VMEM_LIMIT),
        cost_estimate=pl.CostEstimate(
            flops=4 * rows * pairs * 2 * seq * seq * 256,
            bytes_accessed=rows * seq * model * 12,
            transcendentals=rows * pairs * 2 * seq * seq,
        ),
        name="attn_fwd",
    )(q, k, v, e, f)


def attn_backward(qb, k, v, f, dctx, ctx):
    rows, seq, model = k.shape
    pairs = model // 128
    wide = pl.BlockSpec((1, seq, 128), lambda r, p: (r, 0, p))
    mask = pl.BlockSpec((1, seq, 128), lambda r, p: (r, 0, 0))
    out = jax.ShapeDtypeStruct((rows, seq, model), BF)
    return pl.pallas_call(
        attn_bwd_kernel,
        grid=(rows, pairs),
        in_specs=[pl.BlockSpec((1, 2, seq, 128), lambda r, p: (r, p, 0, 0)), wide, wide, mask, wide, wide],
        out_specs=[wide, wide, wide],
        out_shape=[out, out, out],
        compiler_params=pltpu.CompilerParams(vmem_limit_bytes=VMEM_LIMIT),
        cost_estimate=pl.CostEstimate(
            flops=10 * rows * pairs * 2 * seq * seq * 256,
            bytes_accessed=rows * seq * model * 18,
            transcendentals=rows * pairs * 2 * seq * seq,
        ),
        name="attn_bwd",
    )(qb, k, v, f, dctx, ctx)


def gelu_pair(x):
    mag = jnp.abs(x)
    bell = jnp.exp(-0.5 * x * x)
    t = 1.0 / (1.0 + 0.23164189 * mag)
    poly = t * (0.127414796 + t * (-0.142248368 + t * (0.7107068705 + t * (-0.7265760135 + t * 0.5307027145))))
    tail = poly * bell
    cdf = jnp.where(x >= 0, 1.0 - tail, tail)
    return x * cdf, cdf + x * (bell * 0.3989422804)


def norm_parts(value):
    center = value - jnp.mean(value, axis=-1, keepdims=True)
    spread = jnp.mean(center * center, axis=-1, keepdims=True)
    inv = lax.rsqrt(spread + 1e-12)
    return center * inv, inv


def norm_back(grad, gain, unit, inv):
    scaled = grad * gain
    mean = jnp.mean(scaled, axis=-1, keepdims=True)
    along = jnp.mean(scaled * unit, axis=-1, keepdims=True)
    return inv * (scaled - mean - unit * along)


def add(a, b):
    return (a.astype(F32) + b.astype(F32)).astype(BF)


def scatter_stages(first):
    wide, blk = lax.axis_size("wide"), lax.axis_size("blk")
    across = [("wide", 1), ("blk", 2)] if first == "x" else [("blk", 2), ("wide", 1)]
    stages = [("blk", 1)] + across + [("wide", 2), ("wide", 4)]
    rest = [("wide", 1 << i) for i in range(3, wide.bit_length() - 1)]
    rest += [("blk", 1 << i) for i in range(2, blk.bit_length() - 1)]
    return stages, rest


def bit_of(axis, mask):
    return jnp.where((lax.axis_index(axis) & mask) != 0, 1, 0)


def reduce_scatter(value, first):
    stages, rest = scatter_stages(first)
    for axis, mask in stages:
        half = value.shape[0] // 2
        bit = bit_of(axis, mask)
        send = lax.dynamic_slice_in_dim(value, (1 - bit) * half, half, 0)
        keep = lax.dynamic_slice_in_dim(value, bit * half, half, 0)
        value = add(keep, swap(send, axis, mask))
    for axis, mask in rest:
        value = add(value, swap(value, axis, mask))
    return value


def gather(value, first):
    stages, _ = scatter_stages(first)
    for axis, mask in reversed(stages):
        value = jnp.concatenate([value, swap(value, axis, mask)], axis=0)
    return value


def place_kernel(me_ref, value_ref, out_ref, *, piece):
    low = me_ref[0] & 3
    for i in range(4):
        at = pl.multiple_of((i ^ low) * piece, 8)
        out_ref[i * piece : (i + 1) * piece, :] = value_ref[pl.ds(at, piece), :].astype(F32)


def place(value, first):
    stages, _ = scatter_stages(first)
    me = jnp.int32(0)
    for axis, mask in stages:
        me = me * 2 + bit_of(axis, mask)
    pieces = 1 << len(stages)
    rows, cols = value.shape
    piece = rows // pieces
    group = 4 * piece
    return pl.pallas_call(
        functools.partial(place_kernel, piece=piece),
        grid_spec=pltpu.PrefetchScalarGridSpec(
            num_scalar_prefetch=1,
            grid=(pieces // 4,),
            in_specs=[pl.BlockSpec((group, cols), lambda i, m: (i ^ (m[0] >> 2), 0))],
            out_specs=pl.BlockSpec((group, cols), lambda i, m: (i, 0)),
        ),
        out_shape=jax.ShapeDtypeStruct((rows, cols), F32),
        compiler_params=pltpu.CompilerParams(vmem_limit_bytes=VMEM_LIMIT),
        cost_estimate=pl.CostEstimate(flops=0, bytes_accessed=rows * cols * 6, transcendentals=0),
        name="place",
    )(me.reshape(1).astype(jnp.int32), value)


def sum_all(value, first):
    return place(gather(reduce_scatter(value, first), first), first)


def butterfly(value):
    for axis in ("blk", "wide"):
        for i in range(lax.axis_size(axis).bit_length() - 1):
            value = value + swap(value, axis, 1 << i)
    return value


def to_rows(value):
    parts = lax.axis_size("blk")
    rows, width, model = value.shape
    own = rows // parts
    me = lax.axis_index("blk")
    got = []
    for j in range(parts):
        piece = lax.dynamic_slice_in_dim(value, (me ^ j) * own, own, 0)
        got.append(swap(piece, "blk", j) if j else piece)
    return jnp.stack(got, axis=1).reshape(own, parts * width, model)


def from_rows(value, width):
    parts = lax.axis_size("blk")
    own, _, model = value.shape
    value = value.reshape(own, parts, width, model)
    me = lax.axis_index("blk")
    out = jnp.zeros((own * parts, width, model), value.dtype)
    for j in range(parts):
        piece = value[:, j]
        got = swap(piece, "blk", j) if j else piece
        out = lax.dynamic_update_slice_in_dim(out, got, (me ^ j) * own, 0)
    return out


def mask_lanes(lengths, own, width):
    parts = lax.axis_size("blk")
    me = lax.axis_index("blk")
    mine = lax.dynamic_slice_in_dim(lengths, me * own, own, 0)
    ends = jnp.cumsum(mine, axis=-1)
    start = (me ^ jnp.arange(parts, dtype=jnp.int32)) * width
    place_of = (start[:, None] + jnp.arange(width, dtype=jnp.int32)[None, :]).reshape(-1)
    seg = jnp.sum((place_of[None, :, None] >= ends[:, None, :]).astype(jnp.int32), axis=-1)
    lane = jnp.arange(128, dtype=jnp.int32) % 64
    same = seg[:, :, None] == lane
    docs = lane < 8
    e = jnp.where(same & docs, 1.0, 0.0).astype(BF)
    f = jnp.where(docs & ~same, -BIG, jnp.where((lane >= 8) & (lane < 11), -1.0, 0.0)).astype(BF)
    return e, f


def per_device(
    tokens,
    lengths,
    query_weight,
    query_bias,
    key_weight,
    value_weight,
    value_bias,
    out_weight,
    out_bias,
    first_gain,
    first_shift,
    inner_weight,
    inner_bias,
    outer_weight,
    outer_bias,
    second_gain,
    second_shift,
    cotangent,
):
    rows_dev, width, model = tokens.shape
    parts = lax.axis_size("blk")
    rows, seq = rows_dev // parts, parts * width
    count = rows * seq
    shape3 = (rows, seq, model)
    f32 = lambda item: item.astype(F32)

    x = to_rows(tokens).reshape(count, model)
    pull = to_rows(cotangent).reshape(count, model)
    e, f = mask_lanes(lengths, rows, width)

    q = (matmul(x, query_weight) + f32(query_bias)).astype(BF)
    k = matmul(x, key_weight).astype(BF)
    v = (matmul(x, value_weight) + f32(value_bias)).astype(BF)
    q, k, v = (item.reshape(shape3) for item in (q, k, v))
    ctx3, qb = attn_forward(q, k, v, e, f)
    ctx = ctx3.reshape(count, model)
    z1 = f32(x) + matmul(ctx, out_weight) + f32(out_bias)
    unit1, inv1 = norm_parts(z1)
    y1 = unit1 * f32(first_gain) + f32(first_shift)
    y1_low = y1.astype(BF)
    hidden = matmul(y1_low, inner_weight) + f32(inner_bias)
    gel, slope = gelu_pair(hidden)
    gel = gel.astype(BF)
    slope = slope.astype(BF)
    z2 = y1 + matmul(gel, outer_weight) + f32(outer_bias)
    unit2, inv2 = norm_parts(z2)
    output = (unit2 * f32(second_gain) + f32(second_shift)).astype(BF)
    output = from_rows(output.reshape(shape3), width)

    g = f32(pull)
    grad_g2 = jnp.sum(g * unit2, axis=0)
    grad_e2 = jnp.sum(g, axis=0)
    dz2 = norm_back(g, f32(second_gain), unit2, inv2)
    dff = dz2.astype(BF)
    grad_w2 = dot_tn(gel, dff).astype(BF)
    grad_c2 = jnp.sum(f32(dff), axis=0)
    dh = (dot_nt(dff, outer_weight) * f32(slope)).astype(BF)
    grad_w1 = dot_tn(y1_low, dh).astype(BF)
    grad_c1 = jnp.sum(f32(dh), axis=0)
    dy1 = dz2 + dot_nt(dh, inner_weight)
    grad_g1 = jnp.sum(dy1 * unit1, axis=0)
    grad_e1 = jnp.sum(dy1, axis=0)
    dz1 = norm_back(dy1, f32(first_gain), unit1, inv1)
    da = dz1.astype(BF)
    grad_wo = dot_tn(ctx, da).astype(BF)
    grad_bo = jnp.sum(f32(da), axis=0)
    dctx = dot_nt(da, out_weight).astype(BF).reshape(shape3)
    dq, dk, dv = attn_backward(qb, k, v, f, dctx, ctx3)
    dq, dk, dv = (item.reshape(count, model) for item in (dq, dk, dv))
    grad_wq = dot_tn(x, dq).astype(BF)
    grad_wk = dot_tn(x, dk).astype(BF)
    grad_wv = dot_tn(x, dv).astype(BF)
    grad_bq = jnp.sum(f32(dq), axis=0)
    grad_bv = jnp.sum(f32(dv), axis=0)
    dx = dz1 + dot_nt(dq, query_weight) + dot_nt(dk, key_weight) + dot_nt(dv, value_weight)
    grad_tokens = from_rows(dx.astype(BF).reshape(shape3), width)

    grad_w2 = sum_all(grad_w2, "x")
    grad_w1 = sum_all(grad_w1, "y")
    grad_wo = sum_all(grad_wo, "x")
    grad_wq = sum_all(grad_wq, "y")
    grad_wk = sum_all(grad_wk, "x")
    grad_wv = sum_all(grad_wv, "y")
    small = (grad_bq, grad_bv, grad_bo, grad_g1, grad_e1, grad_c1, grad_c2, grad_g2, grad_e2)
    joined = butterfly(jnp.concatenate(small))
    cuts = []
    at = 0
    for item in small:
        cuts.append(joined[at : at + item.shape[0]])
        at += item.shape[0]
    grad_bq, grad_bv, grad_bo, grad_g1, grad_e1, grad_c1, grad_c2, grad_g2, grad_e2 = cuts
    return (
        output,
        grad_tokens,
        grad_wq,
        grad_bq,
        grad_wk,
        grad_wv,
        grad_bv,
        grad_wo,
        grad_bo,
        grad_g1,
        grad_e1,
        grad_w1,
        grad_c1,
        grad_w2,
        grad_c2,
        grad_g2,
        grad_e2,
    )


def solution(mesh):
    placed = (P("wide", "blk", None), P("wide", None)) + (P(),) * 15 + (P("wide", "blk", None),)
    return jax.shard_map(
        per_device,
        mesh=mesh,
        in_specs=placed,
        out_specs=(P("wide", "blk", None),) * 2 + (P(),) * 15,
        check_vma=False,
    )
```

time: 1810 us -> 535 us (0.30); the launches traced: 1780 us -> 529 us
  blocking collectives: 456 us -> 0 us
  local copies, waits for them, and re-layouts: 490 us -> 49 us
  other arithmetic: 346 us -> 30.3 us
  matrix products: 208 us -> 105 us
  waiting for transfers between devices: 265 us -> 174 us
  starting transfers between devices: 0.12 us -> 87.4 us
  Pallas kernels: 0 us -> 81.8 us
    unnamed x1 -> x0, blocking collectives: 456 us -> none
    convert_element_type x10 -> x36, other arithmetic: 306 us -> 16 us  [the longest x10 8.61 us: per_device(): f32 = lambda item: item.astype(F32)]
    unnamed x137 -> x116, local copies, waits for them, and re-layouts: 300 us -> 21.9 us
    all_gather x2 -> x0, waiting for transfers between devices: 235 us -> none  [the longest x1 161 us: per_device(): lax.all_gather(mine.astype(jnp.bfloat16), ('wide', 'blk'), axis=0, tiled=...]
    ppermute x0 -> x77, waiting for transfers between devices: none -> 174 us  [swap(): return lax.ppermute(value, axis, [(i, i ^ mask) for i in range(size)])]
    dot_general x24 -> x18, matrix products: 208 us -> 105 us  [the longest x6 48.7 us: dot_nt(): lax.dot_general(left, right, (((1,), (1,)), ((), ())), preferred_element_...]
    ppermute x0 -> x77, starting transfers between devices: none -> 87.4 us  [swap(): return lax.ppermute(value, axis, [(i, i ^ mask) for i in range(size)])]
    slice x10 -> x2, local copies, waits for them, and re-layouts: 87.3 us -> 1.23 us  [per_device(): cuts.append(joined[at:at + item.shape[0]])]
  transfers between devices with their start and end apart: 3 -> 77, of which waited for: 3 -> 35; matrix products, arithmetic and copies ran while one was open for 5% -> 12% of each run, Pallas kernels for 0% -> 6%
where the time goes in v1:
time: 535 us; the launch traced here: 529 us
  waiting for transfers between devices  174 us (33%)
  matrix products  105 us (20%)
  starting transfers between devices  87.4 us (16%)
  Pallas kernels  81.8 us (15%)
  local copies, waits for them, and re-layouts  49 us (9%)
  other arithmetic  30.3 us (6%)
    ppermute x77, waiting for transfers between devices, swap(): return lax.ppermute(value, axis, [(i, i ^ mask) for i in range(size)])  174 us
    ppermute x77, starting transfers between devices, swap(): return lax.ppermute(value, axis, [(i, i ^ mask) for i in range(size)])  87.4 us
    dot_general x6, matrix products, dot_nt(): lax.dot_general(left, right, (((1,), (1,)), ((), ())), preferred_element_...  48.7 us
    pallas_call x6, Pallas kernels, place(): pl.pallas_call(functools.partial(place_kernel, piece=piece), grid_spec=pl...  37.3 us
    dot_general x6, matrix products, matmul(): return jnp.dot(left, right, preferred_element_type=F32)  32.9 us
    dot_general x6, matrix products, dot_tn(): lax.dot_general(left, right, (((0,), (0,)), ((), ())), preferred_element_...  23.3 us
    pallas_call x1, Pallas kernels, attn_forward(): pl.pallas_call(attn_fwd_kernel, grid=(rows, pairs), in_specs=[wide, wide,...  22.6 us
    unnamed x116, local copies, waits for them, and re-layouts  21.9 us
  transfers between devices with their start and end apart: 77, of which 35 were waited for; matrix products, arithmetic and copies ran while one was open for 12% of the time, Pallas kernels for 6%

profile of v1, /device:TPU:0, one launch (start us, length us, event | category | flops | bytes accessed | tf_op | source)
XLA Modules:
  0.0 529.5 jit_solution(7671145033230525044)
XLA Ops:
  25.5 6.8 %collective-permute-done.2 = bf16[2,128,768]{2,1,0:T(8,128)(2,1)S(1)} collective-permute-done((bf16[2,128,768]{2,1,0:T(8,128)(2,1)}, bf16[2,128,768]{2,1,0:T(8,128)(2,1)S(1)}, u32[]{:S(2)}, u32[]{:S(2)}) %collective-permute-start.2) | collective-permute-done | bytes 393248 | tf_op jit(solution)/shard_map/ppermute | solution.py:19
  32.3 8.6 %collective-permute-done.1 = bf16[2,128,768]{2,1,0:T(8,128)(2,1)} collective-permute-done((bf16[2,128,768]{2,1,0:T(8,128)(2,1)}, bf16[2,128,768]{2,1,0:T(8,128)(2,1)}, u32[]{:S(2)}, u32[]{:S(2)}) %collective-permute-start.1) | collective-permute-done | bytes 393248 | tf_op jit(solution)/shard_map/ppermute | solution.py:19
  51.0 22.6 %attn_fwd.1 = (bf16[2,512,768]{2,1,0:T(8,128)(2,1)}, bf16[2,12,512,128]{3,2,1,0:T(8,128)(2,1)}) custom-call(bf16[2,512,768]{2,1,0:T(8,128)(2,1)} %bitcast.139, bf16[2,512,768]{2,1,0:T(8,128)(2,1)} %bitcast.132, bf16[2,512,768]{2,1,0:T(8,128)(2,1)} %bitcast.134, bf16[2,512,128]{2,1,0:T(8,128)(2,1)} %select_convert_fusion.1.e_ref, ...), custom_call_target="tpu_custom_call" | custom-call | flops 6442450944 | bytes 9437184 | tf_op jit(solution)/shard_map/attn_fwd/pallas_call | solution.py:101
  77.5 16.8 %multiply_convert_fusion.1 = (bf16[1024,3072]{1,0:T(8,128)(2,1)S(1)}, f32[1024,3072]{1,0:T(8,128)}) fusion(f32[3072]{0:T(1024)S(1)} %copy-done.23, bf16[768,3072]{1,0:T(8,128)(2,1)S(1)} %bitcast.129, f32[1024,768]{1,0:T(8,128)S(1)} %get-tuple-element.123, f32[768]{0:T(1024)S(1)} %copy-done.25, f32[768]{0:T(1024)S(1)} %convert_element_type.405, ...), kind=kOutput, calls=%fused_computation.6 | convolution fusion | flops 4904976384 | bytes 26765312 | tf_op jit(solution)/shard_map/dot_general | solution.py:23
  94.4 5.4 %fusion.17 = (f32[1024]{0:T(1024)S(1)}, f32[1024,768]{1,0:T(8,128)S(1)}) fusion(f32[768]{0:T(1024)S(1)} %copy-done.26, bf16[1024,3072]{1,0:T(8,128)(2,1)S(1)} %get-tuple-element.124, bf16[3072,768]{1,0:T(8,128)(2,1)S(1)} %bitcast.127, f32[768]{0:T(1024)S(1)} %copy-done.25, f32[768]{0:T(1024)S(1)} %convert_element_type.405, f32[1024]{0:T(1024)S(1)} %add_rsqrt_fusion.1, ...), kind=kOutput, calls=%fused_computation.253 | convolution fusion | flops 4837342208 | bytes 17323008 | tf_op jit(solution)/shard_map/dot_general | solution.py:23
  103.9 18.7 %convert_reduce_fusion = (f32[3072]{0:T(1024)S(1)}, bf16[1024,3072]{1,0:T(8,128)(2,1)}) fusion(f32[1024,3072]{1,0:T(8,128)} %get-tuple-element.125, f32[3072]{0:T(1024)S(1)} %copy-done.23, bf16[3072,768]{1,0:T(8,128)(2,1)} %param.31, f32[1024,768]{1,0:T(8,128)S(1)} %get-tuple-element.46), kind=kOutput, calls=%fused_computation.3 | convolution fusion | flops 4923847680 | bytes 26763264 | tf_op jit(solution)/shard_map/dot_general | solution.py:27
  122.6 21.5 %multiply_reduce_fusion = (f32[768]{0:T(1024)S(1)}, f32[1024]{0:T(1024)S(1)}, f32[1024]{0:T(1024)S(1)}, f32[768]{0:T(1024)S(1)}, f32[1024,768]{1,0:T(8,128)S(1)}) fusion(f32[1024,768]{1,0:T(8,128)S(1)} %get-tuple-element.123, f32[1024]{0:T(1024)S(1)} %add_rsqrt_fusion.1, f32[1024]{0:T(1024)S(1)} %broadcast_multiply_fusion.4, ...), kind=kOutput, calls=%fused_computation.18 | convolution fusion | flops 4839698432 | bytes 20472832 | tf_op jit(solution)/shard_map/dot_general | solution.py:27
  147.8 21.9 %attn_bwd.1 = (bf16[2,512,768]{2,1,0:T(8,128)(2,1)}, bf16[2,512,768]{2,1,0:T(8,128)(2,1)}, bf16[2,512,768]{2,1,0:T(8,128)(2,1)}) custom-call(bf16[2,12,512,128]{3,2,1,0:T(8,128)(2,1)} %get-tuple-element.23.qb_ref, bf16[2,512,768]{2,1,0:T(8,128)(2,1)} %bitcast.133, bf16[2,512,768]{2,1,0:T(8,128)(2,1)} %bitcast.135, ...), custom_call_target="tpu_custom_call" | custom-call | flops 16106127360 | bytes 14155776 | tf_op jit(solution)/shard_map/attn_bwd/pallas_call | solution.py:126
  179.3 8.7 %convolution_convert_fusion.1 = bf16[768,3072]{1,0:T(8,128)(2,1)S(1)} fusion(bf16[1024,3072]{1,0:T(8,128)(2,1)} %get-tuple-element.130, f32[1024,768]{1,0:T(8,128)S(1)} %copy-done.3, f32[768]{0:T(1024)S(1)} %copy-done.25, f32[768]{0:T(1024)S(1)} %convert_element_type.405, f32[1024]{0:T(1024)S(1)} %add_rsqrt_fusion.1, f32[1024]{0:T(1024)S(1)} %broadcast_multiply_fusion.4), kind=kOutput, calls=%fused_computation.11 | convolution fusion | flops 4838129664 | bytes 14170112 | tf_op jit(solution)/shard_map/dot_general | solution.py:31
  188.0 8.8 %convolution_convert_fusion = bf16[3072,768]{1,0:T(8,128)(2,1)S(1)} fusion(bf16[1024,3072]{1,0:T(8,128)(2,1)} %copy-done.37, f32[1024,768]{1,0:T(8,128)S(1)} %copy-done.8), kind=kOutput, calls=%fused_computation.10 | convolution fusion | flops 4834983936 | bytes 14155776 | tf_op jit(solution)/shard_map/dot_general | solution.py:31
  208.5 10.0 %collective-permute-done.23 = f32[9216]{0:T(1024)S(1)} collective-permute-done((f32[9216]{0:T(1024)S(1)}, f32[9216]{0:T(1024)S(1)}, u32[]{:S(2)}, u32[]{:S(2)}) %collective-permute-start.23) | collective-permute-done | bytes 36896 | tf_op jit(solution)/shard_map/ppermute | solution.py:19
  239.8 10.7 %collective-permute-done.13 = bf16[192,768]{1,0:T(8,128)(2,1)S(1)} collective-permute-done((bf16[192,768]{1,0:T(8,128)(2,1)S(1)}, bf16[192,768]{1,0:T(8,128)(2,1)S(1)}, u32[]{:S(2)}, u32[]{:S(2)}) %collective-permute-start.13) | collective-permute-done | bytes 294944 | tf_op jit(solution)/shard_map/ppermute | solution.py:19
  253.9 5.3 %collective-permute-done.38 = bf16[192,768]{1,0:T(8,128)(2,1)S(1)} collective-permute-done((bf16[192,768]{1,0:T(8,128)(2,1)S(1)}, bf16[192,768]{1,0:T(8,128)(2,1)S(1)}, u32[]{:S(2)}, u32[]{:S(2)}) %collective-permute-start.38) | collective-permute-done | bytes 294944 | tf_op jit(solution)/shard_map/ppermute | solution.py:19
  319.0 12.5 %collective-permute-done.58 = bf16[192,3072]{1,0:T(8,128)(2,1)S(1)} collective-permute-done((bf16[192,3072]{1,0:T(8,128)(2,1)S(1)}, bf16[192,3072]{1,0:T(8,128)(2,1)S(1)}, u32[]{:S(2)}, u32[]{:S(2)}) %collective-permute-start.58) | collective-permute-done | bytes 1179680 | tf_op jit(solution)/shard_map/ppermute | solution.py:19
  334.1 9.6 %collective-permute-done.68 = bf16[768,768]{1,0:T(8,128)(2,1)S(1)} collective-permute-done((bf16[768,768]{1,0:T(8,128)(2,1)S(1)}, bf16[768,768]{1,0:T(8,128)(2,1)S(1)}, u32[]{:S(2)}, u32[]{:S(2)}) %collective-permute-start.68) | collective-permute-done | bytes 1179680 | tf_op jit(solution)/shard_map/ppermute | solution.py:19
  351.4 8.5 %collective-permute-done.69 = bf16[384,768]{1,0:T(8,128)(2,1)S(1)} collective-permute-done((bf16[384,768]{1,0:T(8,128)(2,1)S(1)}, bf16[384,768]{1,0:T(8,128)(2,1)S(1)}, u32[]{:S(2)}, u32[]{:S(2)}) %collective-permute-start.69) | collective-permute-done | bytes 589856 | tf_op jit(solution)/shard_map/ppermute | solution.py:19
  361.5 5.4 %collective-permute-done.60 = bf16[48,3072]{1,0:T(8,128)(2,1)S(1)} collective-permute-done((bf16[48,3072]{1,0:T(8,128)(2,1)S(1)}, bf16[48,3072]{1,0:T(8,128)(2,1)S(1)}, u32[]{:S(2)}, u32[]{:S(2)}) %collective-permute-start.60) | collective-permute-done | bytes 294944 | tf_op jit(solution)/shard_map/ppermute | solution.py:19
  368.5 6.1 %collective-permute-done.70 = bf16[192,768]{1,0:T(8,128)(2,1)S(1)} collective-permute-done((bf16[192,768]{1,0:T(8,128)(2,1)S(1)}, bf16[192,768]{1,0:T(8,128)(2,1)S(1)}, u32[]{:S(2)}, u32[]{:S(2)}) %collective-permute-start.70) | collective-permute-done | bytes 294944 | tf_op jit(solution)/shard_map/ppermute | solution.py:19
  376.3 8.2 %collective-permute-done.61 = bf16[24,3072]{1,0:T(8,128)(2,1)S(1)} collective-permute-done((bf16[24,3072]{1,0:T(8,128)(2,1)S(1)}, bf16[24,3072]{1,0:T(8,128)(2,1)S(1)}, u32[]{:S(2)}, u32[]{:S(2)}) %collective-permute-start.61) | collective-permute-done | bytes 147488 | tf_op jit(solution)/shard_map/ppermute | solution.py:19
  385.2 6.4 %collective-permute-done.71 = bf16[96,768]{1,0:T(8,128)(2,1)S(1)} collective-permute-done((bf16[96,768]{1,0:T(8,128)(2,1)S(1)}, bf16[96,768]{1,0:T(8,128)(2,1)S(1)}, u32[]{:S(2)}, u32[]{:S(2)}) %collective-permute-start.71) | collective-permute-done | bytes 147488 | tf_op jit(solution)/shard_map/ppermute | solution.py:19
  392.6 5.9 %collective-permute-done.62 = bf16[24,3072]{1,0:T(8,128)(2,1)S(1)} collective-permute-done((bf16[24,3072]{1,0:T(8,128)(2,1)S(1)}, bf16[24,3072]{1,0:T(8,128)(2,1)S(1)}, u32[]{:S(2)}, u32[]{:S(2)}) %collective-permute-start.62) | collective-permute-done | bytes 147488 | tf_op jit(solution)/shard_map/ppermute | solution.py:19
  413.5 9.6 %collective-permute-done.64 = bf16[96,3072]{1,0:T(8,128)(2,1)S(1)} collective-permute-done((bf16[96,3072]{1,0:T(8,128)(2,1)S(1)}, bf16[96,3072]{1,0:T(8,128)(2,1)S(1)}, u32[]{:S(2)}, u32[]{:S(2)}) %collective-permute-start.64) | collective-permute-done | bytes 589856 | tf_op jit(solution)/shard_map/ppermute | solution.py:19
  427.9 11.5 %collective-permute-done.65 = bf16[192,3072]{1,0:T(8,128)(2,1)S(1)} collective-permute-done((bf16[192,3072]{1,0:T(8,128)(2,1)S(1)}, bf16[192,3072]{1,0:T(8,128)(2,1)S(1)}, u32[]{:S(2)}, u32[]{:S(2)}) %collective-permute-start.65) | collective-permute-done | bytes 1179680 | tf_op jit(solution)/shard_map/ppermute | solution.py:19
  447.0 5.2 collective-permute-done.20
  461.4 5.1 collective-permute-done.45
  470.2 5.0 collective-permute-done.55
  479.8 5.5 %place.6 = f32[768,768]{1,0:T(8,128)} custom-call(s32[1]{0:T(128)} %bitcast.30.me_ref, bf16[768,768]{1,0:T(8,128)(2,1)} %constant_dynamic-update-slice_fusion.5.value_ref), custom_call_target="tpu_custom_call" | custom-call | bytes 3538944 | tf_op jit(solution)/shard_map/place/pallas_call | solution.py:219
  487.5 5.5 %place.8 = f32[768,768]{1,0:T(8,128)} custom-call(s32[1]{0:T(128)} %bitcast.30.me_ref, bf16[768,768]{1,0:T(8,128)(2,1)} %copy-done.14), custom_call_target="tpu_custom_call" | custom-call | bytes 3538944 | tf_op jit(solution)/shard_map/place/pallas_call | solution.py:219
  495.0 5.5 %place.7 = f32[768,768]{1,0:T(8,128)} custom-call(s32[1]{0:T(128)} %bitcast.31.me_ref, bf16[768,768]{1,0:T(8,128)(2,1)} %constant_dynamic-update-slice_fusion.17.value_ref), custom_call_target="tpu_custom_call" | custom-call | bytes 3538944 | tf_op jit(solution)/shard_map/place/pallas_call | solution.py:219
  502.6 5.5 %place.9 = f32[768,768]{1,0:T(8,128)} custom-call(s32[1]{0:T(128)} %bitcast.31.me_ref, bf16[768,768]{1,0:T(8,128)(2,1)} %copy-done.17), custom_call_target="tpu_custom_call" | custom-call | bytes 3538944 | tf_op jit(solution)/shard_map/place/pallas_call | solution.py:219
  510.4 7.6 %place.10 = f32[768,3072]{1,0:T(8,128)} custom-call(s32[1]{0:T(128)} %bitcast.30.me_ref, bf16[768,3072]{1,0:T(8,128)(2,1)} %copy-done.5), custom_call_target="tpu_custom_call" | custom-call | bytes 14155776 | tf_op jit(solution)/shard_map/place/pallas_call | solution.py:219
  521.3 7.7 %place.11 = f32[3072,768]{1,0:T(8,128)} custom-call(s32[1]{0:T(128)} %bitcast.31.me_ref, bf16[3072,768]{1,0:T(8,128)(2,1)} %constant_dynamic-update-slice_fusion.61.value_ref), custom_call_target="tpu_custom_call" | custom-call | bytes 14155776 | tf_op jit(solution)/shard_map/place/pallas_call | solution.py:219
  (418 shorter events, 224.9 us)
Async XLA Ops:
  3.3 20.1 %collective-permute-start.8 = (bf16[2,128,768]{2,1,0:T(8,128)(2,1)}, bf16[2,128,768]{2,1,0:T(8,128)(2,1)S(1)}, u32[]{:S(2)}, u32[]{:S(2)}) collective-permute-start(bf16[2,128,768]{2,1,0:T(8,128)(2,1)} %get-tuple-element.57), channel_id=1, source_target_pairs={{0,3},{1,2},{2,1},{3,0},{4,7},{5,6},{6,5},{7,4},{8,11},{9,10},{10,... | collective-permute-start | bytes 1179656 | tf_op jit(solution)/shard_map/ppermute | solution.py:19
  5.7 19.3 %collective-permute-start.7 = (bf16[2,128,768]{2,1,0:T(8,128)(2,1)}, bf16[2,128,768]{2,1,0:T(8,128)(2,1)S(1)}, u32[]{:S(2)}, u32[]{:S(2)}) collective-permute-start(bf16[2,128,768]{2,1,0:T(8,128)(2,1)} %get-tuple-element.58), channel_id=1, source_target_pairs={{0,2},{1,3},{2,0},{3,1},{4,6},{5,7},{6,4},{7,5},{8,10},{9,11},{10,... | collective-permute-start | bytes 1179656 | tf_op jit(solution)/shard_map/ppermute | solution.py:19
  6.3 18.7 %collective-permute-start.6 = (bf16[2,128,768]{2,1,0:T(8,128)(2,1)}, bf16[2,128,768]{2,1,0:T(8,128)(2,1)S(1)}, u32[]{:S(2)}, u32[]{:S(2)}) collective-permute-start(bf16[2,128,768]{2,1,0:T(8,128)(2,1)} %get-tuple-element.56), channel_id=1, source_target_pairs={{0,1},{1,0},{2,3},{3,2},{4,5},{5,4},{6,7},{7,6},{8,9},{9,8},{10,11... | collective-permute-start | bytes 1179656 | tf_op jit(solution)/shard_map/ppermute | solution.py:19
  7.4 25.0 %collective-permute-start.2 = (bf16[2,128,768]{2,1,0:T(8,128)(2,1)}, bf16[2,128,768]{2,1,0:T(8,128)(2,1)S(1)}, u32[]{:S(2)}, u32[]{:S(2)}) collective-permute-start(bf16[2,128,768]{2,1,0:T(8,128)(2,1)} %get-tuple-element.64), channel_id=1, source_target_pairs={{0,3},{1,2},{2,1},{3,0},{4,7},{5,6},{6,5},{7,4},{8,11},{9,10},{10,... | collective-permute-start | bytes 1179656 | tf_op jit(solution)/shard_map/ppermute | solution.py:19
  8.8 32.1 %collective-permute-start.1 = (bf16[2,128,768]{2,1,0:T(8,128)(2,1)}, bf16[2,128,768]{2,1,0:T(8,128)(2,1)}, u32[]{:S(2)}, u32[]{:S(2)}) collective-permute-start(bf16[2,128,768]{2,1,0:T(8,128)(2,1)} %get-tuple-element.65), channel_id=1, source_target_pairs={{0,2},{1,3},{2,0},{3,1},{4,6},{5,7},{6,4},{7,5},{8,10},{9,11},{10,... | collective-permute-start | bytes 1179656 | tf_op jit(solution)/shard_map/ppermute | solution.py:19
  23.4 17.5 %collective-permute-start = (bf16[2,128,768]{2,1,0:T(8,128)(2,1)}, bf16[2,128,768]{2,1,0:T(8,128)(2,1)S(1)}, u32[]{:S(2)}, u32[]{:S(2)}) collective-permute-start(bf16[2,128,768]{2,1,0:T(8,128)(2,1)} %get-tuple-element.63), channel_id=1, source_target_pairs={{0,1},{1,0},{2,3},{3,2},{4,5},{5,4},{6,7},{7,6},{8,9},{9,8},{10,11... | collective-permute-start | bytes 1179656 | tf_op jit(solution)/shard_map/ppermute | solution.py:19
  197.1 35.7 %collective-permute-start.3 = (bf16[2,128,768]{2,1,0:T(8,128)(2,1)S(1)}, bf16[2,128,768]{2,1,0:T(8,128)(2,1)S(1)}, u32[]{:S(2)}, u32[]{:S(2)}) collective-permute-start(bf16[2,128,768]{2,1,0:T(8,128)(2,1)S(1)} %get-tuple-element.61), channel_id=1, source_target_pairs={{0,1},{1,0},{2,3},{3,2},{4,5},{5,4},{6,7},{7,6},{8,9},{9,8},{10,11... | collective-permute-start | bytes 1179656 | tf_op jit(solution)/shard_map/ppermute | solution.py:19
  197.2 37.1 %collective-permute-start.4 = (bf16[2,128,768]{2,1,0:T(8,128)(2,1)S(1)}, bf16[2,128,768]{2,1,0:T(8,128)(2,1)S(1)}, u32[]{:S(2)}, u32[]{:S(2)}) collective-permute-start(bf16[2,128,768]{2,1,0:T(8,128)(2,1)S(1)} %get-tuple-element.60), channel_id=1, source_target_pairs={{0,2},{1,3},{2,0},{3,1},{4,6},{5,7},{6,4},{7,5},{8,10},{9,11},{10,... | collective-permute-start | bytes 1179656 | tf_op jit(solution)/shard_map/ppermute | solution.py:19
  199.5 35.1 %collective-permute-start.5 = (bf16[2,128,768]{2,1,0:T(8,128)(2,1)S(1)}, bf16[2,128,768]{2,1,0:T(8,128)(2,1)S(1)}, u32[]{:S(2)}, u32[]{:S(2)}) collective-permute-start(bf16[2,128,768]{2,1,0:T(8,128)(2,1)S(1)} %get-tuple-element.59), channel_id=1, source_target_pairs={{0,3},{1,2},{2,1},{3,0},{4,7},{5,6},{6,5},{7,4},{8,11},{9,10},{10,... | collective-permute-start | bytes 1179656 | tf_op jit(solution)/shard_map/ppermute | solution.py:19
  203.1 32.0 %collective-permute-start.9 = (bf16[2,128,768]{2,1,0:T(8,128)(2,1)S(1)}, bf16[2,128,768]{2,1,0:T(8,128)(2,1)S(1)}, u32[]{:S(2)}, u32[]{:S(2)}) collective-permute-start(bf16[2,128,768]{2,1,0:T(8,128)(2,1)S(1)} %get-tuple-element.54), channel_id=1, source_target_pairs={{0,1},{1,0},{2,3},{3,2},{4,5},{5,4},{6,7},{7,6},{8,9},{9,8},{10,11... | collective-permute-start | bytes 1179656 | tf_op jit(solution)/shard_map/ppermute | solution.py:19
  232.7 222.1 %collective-permute-start.10 = (bf16[2,128,768]{2,1,0:T(8,128)(2,1)S(1)}, bf16[2,128,768]{2,1,0:T(8,128)(2,1)}, u32[]{:S(2)}, u32[]{:S(2)}) collective-permute-start(bf16[2,128,768]{2,1,0:T(8,128)(2,1)S(1)} %get-tuple-element.53), channel_id=1, source_target_pairs={{0,2},{1,3},{2,0},{3,1},{4,6},{5,7},{6,4},{7,5},{8,10},{9,11},{10,... | collective-permute-start | bytes 1179656 | tf_op jit(solution)/shard_map/ppermute | solution.py:19
  236.3 74.4 %collective-permute-start.57 = (bf16[384,3072]{1,0:T(8,128)(2,1)S(1)}, bf16[384,3072]{1,0:T(8,128)(2,1)S(1)}, u32[]{:S(2)}, u32[]{:S(2)}) collective-permute-start(bf16[384,3072]{1,0:T(8,128)(2,1)S(1)} %constant_dynamic-slice_fusion.9), channel_id=1, source_target_pairs={{0,1},{1,0},{2,3},{3,2},{4,5},{5,4},{6,7},{7,6},{8,9},{9,8},{10,11... | collective-permute-start | bytes 7077896 | tf_op jit(solution)/shard_map/ppermute | solution.py:19
  236.7 80.1 %collective-permute-start.67 = (bf16[1536,768]{1,0:T(8,128)(2,1)S(1)}, bf16[1536,768]{1,0:T(8,128)(2,1)S(1)}, u32[]{:S(2)}, u32[]{:S(2)}) collective-permute-start(bf16[1536,768]{1,0:T(8,128)(2,1)S(1)} %constant_dynamic-slice_fusion.4), channel_id=1, source_target_pairs={{0,1},{1,0},{2,3},{3,2},{4,5},{5,4},{6,7},{7,6},{8,9},{9,8},{10,11... | collective-permute-start | bytes 7077896 | tf_op jit(solution)/shard_map/ppermute | solution.py:19
  238.1 14.2 %collective-permute-start.28 = (bf16[192,768]{1,0:T(8,128)(2,1)S(1)}, bf16[192,768]{1,0:T(8,128)(2,1)S(1)}, u32[]{:S(2)}, u32[]{:S(2)}) collective-permute-start(bf16[192,768]{1,0:T(8,128)(2,1)S(1)} %constant_dynamic-slice_fusion.23), channel_id=1, source_target_pairs={{0,4},{4,0},{8,12},{12,8},{16,20},{20,16},{24,28},{28,24},{1,5},{5... | collective-permute-start | bytes 884744 | tf_op jit(solution)/shard_map/ppermute | solution.py:19
  310.7 87.9 %collective-permute-start.19 = (bf16[96,768]{1,0:T(8,128)(2,1)S(1)}, bf16[96,768]{1,0:T(8,128)(2,1)S(1)}, u32[]{:S(2)}, u32[]{:S(2)}) collective-permute-start(bf16[96,768]{1,0:T(8,128)(2,1)S(1)} %pad_maximum_fusion.11), channel_id=1, source_target_pairs={{0,4},{4,0},{8,12},{12,8},{16,20},{20,16},{24,28},{28,24},{1,5},{5... | collective-permute-start | bytes 442376 | tf_op jit(solution)/shard_map/ppermute | solution.py:19
  313.2 18.4 %collective-permute-start.58 = (bf16[192,3072]{1,0:T(8,128)(2,1)S(1)}, bf16[192,3072]{1,0:T(8,128)(2,1)S(1)}, u32[]{:S(2)}, u32[]{:S(2)}) collective-permute-start(bf16[192,3072]{1,0:T(8,128)(2,1)S(1)} %constant_dynamic-slice_fusion.8), channel_id=1, source_target_pairs={{0,2},{1,3},{2,0},{3,1},{4,6},{5,7},{6,4},{7,5},{8,10},{9,11},{10,... | collective-permute-start | bytes 3538952 | tf_op jit(solution)/shard_map/ppermute | solution.py:19
  314.5 86.6 %collective-permute-start.34 = (bf16[96,768]{1,0:T(8,128)(2,1)S(1)}, bf16[96,768]{1,0:T(8,128)(2,1)S(1)}, u32[]{:S(2)}, u32[]{:S(2)}) collective-permute-start(bf16[96,768]{1,0:T(8,128)(2,1)S(1)} %pad_maximum_fusion.12), channel_id=1, source_target_pairs={{0,2},{1,3},{2,0},{3,1},{4,6},{5,7},{6,4},{7,5},{8,10},{9,11},{10,... | collective-permute-start | bytes 442376 | tf_op jit(solution)/shard_map/ppermute | solution.py:19
  317.6 26.1 %collective-permute-start.68 = (bf16[768,768]{1,0:T(8,128)(2,1)S(1)}, bf16[768,768]{1,0:T(8,128)(2,1)S(1)}, u32[]{:S(2)}, u32[]{:S(2)}) collective-permute-start(bf16[768,768]{1,0:T(8,128)(2,1)S(1)} %constant_dynamic-slice_fusion.3), channel_id=1, source_target_pairs={{0,4},{4,0},{8,12},{12,8},{16,20},{20,16},{24,28},{28,24},{1,5},{5... | collective-permute-start | bytes 3538952 | tf_op jit(solution)/shard_map/ppermute | solution.py:19
  332.0 18.0 %collective-permute-start.59 = (bf16[96,3072]{1,0:T(8,128)(2,1)S(1)}, bf16[96,3072]{1,0:T(8,128)(2,1)S(1)}, u32[]{:S(2)}, u32[]{:S(2)}) collective-permute-start(bf16[96,3072]{1,0:T(8,128)(2,1)S(1)} %constant_dynamic-slice_fusion.7), channel_id=1, source_target_pairs={{0,4},{4,0},{8,12},{12,8},{16,20},{20,16},{24,28},{28,24},{1,5},{5... | collective-permute-start | bytes 1769480 | tf_op jit(solution)/shard_map/ppermute | solution.py:19
  343.7 101.1 %collective-permute-start.44 = (bf16[96,768]{1,0:T(8,128)(2,1)S(1)}, bf16[96,768]{1,0:T(8,128)(2,1)S(1)}, u32[]{:S(2)}, u32[]{:S(2)}) collective-permute-start(bf16[96,768]{1,0:T(8,128)(2,1)S(1)} %pad_maximum_fusion.13), channel_id=1, source_target_pairs={{0,4},{4,0},{8,12},{12,8},{16,20},{20,16},{24,28},{28,24},{1,5},{5... | collective-permute-start | bytes 442376 | tf_op jit(solution)/shard_map/ppermute | solution.py:19
  401.1 43.9 %collective-permute-start.54 = (bf16[96,768]{1,0:T(8,128)(2,1)S(1)}, bf16[96,768]{1,0:T(8,128)(2,1)S(1)}, u32[]{:S(2)}, u32[]{:S(2)}) collective-permute-start(bf16[96,768]{1,0:T(8,128)(2,1)S(1)} %pad_maximum_fusion.14), channel_id=1, source_target_pairs={{0,2},{1,3},{2,0},{3,1},{4,6},{5,7},{6,4},{7,5},{8,10},{9,11},{10,... | collective-permute-start | bytes 442376 | tf_op jit(solution)/shard_map/ppermute | solution.py:19
  407.4 15.6 %collective-permute-start.64 = (bf16[96,3072]{1,0:T(8,128)(2,1)S(1)}, bf16[96,3072]{1,0:T(8,128)(2,1)S(1)}, u32[]{:S(2)}, u32[]{:S(2)}) collective-permute-start(bf16[96,3072]{1,0:T(8,128)(2,1)S(1)} %pad_maximum_fusion.3), channel_id=1, source_target_pairs={{0,4},{4,0},{8,12},{12,8},{16,20},{20,16},{24,28},{28,24},{1,5},{5... | collective-permute-start | bytes 1769480 | tf_op jit(solution)/shard_map/ppermute | solution.py:19
  423.1 16.3 %collective-permute-start.65 = (bf16[192,3072]{1,0:T(8,128)(2,1)S(1)}, bf16[192,3072]{1,0:T(8,128)(2,1)S(1)}, u32[]{:S(2)}, u32[]{:S(2)}) collective-permute-start(bf16[192,3072]{1,0:T(8,128)(2,1)S(1)} %pad_maximum_fusion.1), channel_id=1, source_target_pairs={{0,2},{1,3},{2,0},{3,1},{4,6},{5,7},{6,4},{7,5},{8,10},{9,11},{10,... | collective-permute-start | bytes 3538952 | tf_op jit(solution)/shard_map/ppermute | solution.py:19
  425.2 17.2 %collective-permute-start.75 = (bf16[768,768]{1,0:T(8,128)(2,1)S(1)}, bf16[768,768]{1,0:T(8,128)(2,1)S(1)}, u32[]{:S(2)}, u32[]{:S(2)}) collective-permute-start(bf16[768,768]{1,0:T(8,128)(2,1)S(1)} %pad_maximum_fusion.2), channel_id=1, source_target_pairs={{0,4},{4,0},{8,12},{12,8},{16,20},{20,16},{24,28},{28,24},{1,5},{5... | collective-permute-start | bytes 3538952 | tf_op jit(solution)/shard_map/ppermute | solution.py:19
  440.7 67.4 %collective-permute-start.66 = (bf16[384,3072]{1,0:T(8,128)(2,1)}, bf16[384,3072]{1,0:T(8,128)(2,1)S(1)}, u32[]{:S(2)}, u32[]{:S(2)}) collective-permute-start(bf16[384,3072]{1,0:T(8,128)(2,1)} %get-tuple-element.68), channel_id=1, source_target_pairs={{0,1},{1,0},{2,3},{3,2},{4,5},{5,4},{6,7},{7,6},{8,9},{9,8},{10,11... | collective-permute-start | bytes 7077896 | tf_op jit(solution)/shard_map/ppermute | solution.py:19
  444.8 73.3 %collective-permute-start.76 = (bf16[1536,768]{1,0:T(8,128)(2,1)}, bf16[1536,768]{1,0:T(8,128)(2,1)}, u32[]{:S(2)}, u32[]{:S(2)}) collective-permute-start(bf16[1536,768]{1,0:T(8,128)(2,1)} %get-tuple-element.66), channel_id=1, source_target_pairs={{0,1},{1,0},{2,3},{3,2},{4,5},{5,4},{6,7},{7,6},{8,9},{9,8},{10,11... | collective-permute-start | bytes 7077896 | tf_op jit(solution)/shard_map/ppermute | solution.py:19
  445.0 14.8 %collective-permute-start.11 = (bf16[2,128,768]{2,1,0:T(8,128)(2,1)S(1)}, bf16[2,128,768]{2,1,0:T(8,128)(2,1)S(1)}, u32[]{:S(2)}, u32[]{:S(2)}) collective-permute-start(bf16[2,128,768]{2,1,0:T(8,128)(2,1)S(1)} %get-tuple-element.52), channel_id=1, source_target_pairs={{0,3},{1,2},{2,1},{3,0},{4,7},{5,6},{6,5},{7,4},{8,11},{9,10},{10,... | collective-permute-start | bytes 1179656 | tf_op jit(solution)/shard_map/ppermute | solution.py:19
  452.2 14.4 %collective-permute-start.45 = (bf16[192,768]{1,0:T(8,128)(2,1)S(1)}, bf16[192,768]{1,0:T(8,128)(2,1)S(1)}, u32[]{:S(2)}, u32[]{:S(2)}) collective-permute-start(bf16[192,768]{1,0:T(8,128)(2,1)S(1)} %pad_maximum_fusion.7), channel_id=1, source_target_pairs={{0,2},{1,3},{2,0},{3,1},{4,6},{5,7},{6,4},{7,5},{8,10},{9,11},{10,... | collective-permute-start | bytes 884744 | tf_op jit(solution)/shard_map/ppermute | solution.py:19
  459.8 16.1 %collective-permute-start.21 = (bf16[384,768]{1,0:T(8,128)(2,1)S(1)}, bf16[384,768]{1,0:T(8,128)(2,1)S(1)}, u32[]{:S(2)}, u32[]{:S(2)}) collective-permute-start(bf16[384,768]{1,0:T(8,128)(2,1)S(1)} %get-tuple-element.84), channel_id=1, source_target_pairs={{0,1},{1,0},{2,3},{3,2},{4,5},{5,4},{6,7},{7,6},{8,9},{9,8},{10,11... | collective-permute-start | bytes 1769480 | tf_op jit(solution)/shard_map/ppermute | solution.py:19
  469.4 16.0 %collective-permute-start.46 = (bf16[384,768]{1,0:T(8,128)(2,1)}, bf16[384,768]{1,0:T(8,128)(2,1)}, u32[]{:S(2)}, u32[]{:S(2)}) collective-permute-start(bf16[384,768]{1,0:T(8,128)(2,1)} %get-tuple-element.80), channel_id=1, source_target_pairs={{0,1},{1,0},{2,3},{3,2},{4,5},{5,4},{6,7},{7,6},{8,9},{9,8},{10,11... | collective-permute-start | bytes 1769480 | tf_op jit(solution)/shard_map/ppermute | solution.py:19
  475.2 17.8 %collective-permute-start.36 = (bf16[384,768]{1,0:T(8,128)(2,1)}, bf16[384,768]{1,0:T(8,128)(2,1)}, u32[]{:S(2)}, u32[]{:S(2)}) collective-permute-start(bf16[384,768]{1,0:T(8,128)(2,1)} %get-tuple-element.82), channel_id=1, source_target_pairs={{0,1},{1,0},{2,3},{3,2},{4,5},{5,4},{6,7},{7,6},{8,9},{9,8},{10,11... | collective-permute-start | bytes 1769480 | tf_op jit(solution)/shard_map/ppermute | solution.py:19
  475.9 24.5 %collective-permute-start.56 = (bf16[384,768]{1,0:T(8,128)(2,1)}, bf16[384,768]{1,0:T(8,128)(2,1)}, u32[]{:S(2)}, u32[]{:S(2)}) collective-permute-start(bf16[384,768]{1,0:T(8,128)(2,1)} %get-tuple-element.78), channel_id=1, source_target_pairs={{0,1},{1,0},{2,3},{3,2},{4,5},{5,4},{6,7},{7,6},{8,9},{9,8},{10,11... | collective-permute-start | bytes 1769480 | tf_op jit(solution)/shard_map/ppermute | solution.py:19
  (87 other events, 725.1 us)
